TPU v7x, 32 devices: a whole 2x2x4 slice. The times are simulated.
32 devices in a mesh: req: 2 (over x), hst: 16 (over z, y, core).
Axes of the slice: x: 2, y: 2, z: 4, core: 2. Of those that a mesh axis runs over, the one named last changes fastest.
Arguments:
- ctx_q: bfloat16 [4096, 4096], P(('req', 'hst')), parts along dimension 0, may hold values from -24 to 24
- ctx_k: bfloat16 [4096, 512], P(('req', 'hst')), parts along dimension 0, may hold values from -8 to 8
- ctx_v: bfloat16 [4096, 512], P(('req', 'hst')), parts along dimension 0, may hold values from -6 to 6
- ask_q: bfloat16 [64, 4096], P(('req', 'hst')), parts along dimension 0, may hold values from -24 to 24
- ask_k: bfloat16 [64, 512], P(('req', 'hst')), parts along dimension 0, may hold values from -9 to 9
- ask_v: bfloat16 [64, 512], P(('req', 'hst')), parts along dimension 0, may hold values from -6 to 6
- valid: int32 [32], P(('req', 'hst')), parts along dimension 0, may hold values from 64 to 128, as said below
Outputs:
- ctx_out: bfloat16 [4096, 4096], P(('req', 'hst')), parts along dimension 0
- ask_out: bfloat16 [64, 4096], P(('req', 'hst')), parts along dimension 0
There are 2 independent parts, one for each index of `req`. A program takes and returns all parts, laid end to end along the dimension named above; each array names one. Nothing has to cross between parts.
Inputs may be any that keep to these rules, and one draw needn't show every extreme that they name: `valid`: block 0, the anchor, is always full.
All inputs are finite; a program needn't handle non-finite values.
Results may differ from a plain program's by a relative error of at most 0.0029.
Values may be sent and summed in bfloat16 or wider, within the bound.
No kernel may reach another device: no remote copies, remote signals or barrier semaphores. Data moves between devices by JAX's collectives and lax.ppermute only.
A program may use at most 320 MiB of HBM per device.

v0:
```python
import math

import jax
import jax.numpy as jnp
from jax import lax
from jax.sharding import PartitionSpec as P

H = 32
KVH = 4
DH = 128


def from_root(array, axis, root):
    mine = lax.axis_index(axis) == root
    return lax.psum(jnp.where(mine, array, jnp.zeros_like(array)), axis)


def partial_attend(queries, key_rows, value_rows, visible):
    row_count = queries.shape[0]
    group_size = H // KVH
    group_width = group_size * DH
    scale = 1.0 / math.sqrt(DH)

    def one_group(group_index, carry):
        maxima, totals, outputs = carry
        query_part = lax.dynamic_slice_in_dim(queries, group_index * group_width, group_width, 1)
        query_part = query_part.reshape(row_count, group_size, DH)
        key_part = lax.dynamic_slice_in_dim(key_rows, group_index * DH, DH, 1)
        value_part = lax.dynamic_slice_in_dim(value_rows, group_index * DH, DH, 1)
        scores = (
            jnp.einsum("rgd,sd->rgs", query_part, key_part, preferred_element_type=jnp.float32)
            * scale
        )
        scores = jnp.where(visible[:, None, :], scores, -jnp.inf)
        row_max = jnp.max(scores, axis=-1)
        expon = jnp.exp(scores - row_max[..., None])
        row_sum = jnp.sum(expon, axis=-1)
        weights = expon.astype(jnp.bfloat16)
        mixed = jnp.einsum("rgs,sd->rgd", weights, value_part, preferred_element_type=jnp.float32)
        maxima = lax.dynamic_update_slice_in_dim(maxima, row_max, group_index * group_size, 1)
        totals = lax.dynamic_update_slice_in_dim(totals, row_sum, group_index * group_size, 1)
        outputs = lax.dynamic_update_slice_in_dim(
            outputs, mixed.reshape(row_count, group_width), group_index * group_width, 1
        )
        return (maxima, totals, outputs)

    start_carry = (
        jnp.zeros((row_count, H), jnp.float32),
        jnp.zeros((row_count, H), jnp.float32),
        jnp.zeros((row_count, H * DH), jnp.float32),
    )
    return lax.fori_loop(0, KVH, one_group, start_carry)


def weigh(values, factor):
    shape = values.shape
    return (values.reshape(shape[:-1] + (H, DH)) * factor[..., None]).reshape(shape)


def body(ctx_q, ctx_k, ctx_v, ask_q, ask_k, ask_v, valid):
    block_rows = ctx_q.shape[0]
    host_index = lax.axis_index("hst")
    host_count = lax.axis_size("hst")
    valid_count = valid[0]
    local = jnp.arange(block_rows, dtype=jnp.int32)
    anchor_k, anchor_v = (from_root(ctx_k, "hst", 0), from_root(ctx_v, "hst", 0))
    own_visible = (local[None, :] <= local[:, None]) & (local[None, :] < valid_count)
    anchor_visible = jnp.broadcast_to(host_index > 0, (block_rows, block_rows))
    visible = jnp.concatenate([anchor_visible, own_visible], axis=1)
    row_max, row_sum, mixed = partial_attend(
        ctx_q, jnp.concatenate([anchor_k, ctx_k], 0), jnp.concatenate([anchor_v, ctx_v], 0), visible
    )
    normed = weigh(mixed, 1.0 / row_sum)
    ctx_out = jnp.where(local[:, None] < valid_count, normed, 0.0).astype(jnp.bfloat16)
    all_q, all_k, all_v = (
        lax.all_gather(ask_q, "hst", axis=0, tiled=True),
        lax.all_gather(ask_k, "hst", axis=0, tiled=True),
        lax.all_gather(ask_v, "hst", axis=0, tiled=True),
    )
    query_count = all_q.shape[0]
    query_pos = jnp.arange(query_count, dtype=jnp.int32)
    is_last = host_index == host_count - 1
    ask_visible = jnp.concatenate(
        [
            jnp.broadcast_to(local[None, :] < valid_count, (query_count, block_rows)),
            (query_pos[None, :] <= query_pos[:, None]) & is_last,
        ],
        axis=1,
    )
    ask_max, ask_sum, ask_mixed = partial_attend(
        all_q, jnp.concatenate([ctx_k, all_k], 0), jnp.concatenate([ctx_v, all_v], 0), ask_visible
    )
    maxima, totals, outputs = (
        lax.all_to_all(ask_max[None], "hst", split_axis=1, concat_axis=0, tiled=True),
        lax.all_to_all(ask_sum[None], "hst", split_axis=1, concat_axis=0, tiled=True),
        lax.all_to_all(ask_mixed[None], "hst", split_axis=1, concat_axis=0, tiled=True),
    )
    best = jnp.max(maxima, axis=0)
    scaling = jnp.exp(maxima - best[None])
    total = jnp.sum(totals * scaling, axis=0)
    summed = jnp.sum(weigh(outputs, scaling), axis=0)
    ask_out = weigh(summed, 1.0 / total).astype(jnp.bfloat16)
    return (ctx_out, ask_out)


def solution(mesh):
    in_specs = (
        P(("req", "hst"), None),
        P(("req", "hst"), None),
        P(("req", "hst"), None),
        P(("req", "hst"), None),
        P(("req", "hst"), None),
        P(("req", "hst"), None),
        P(("req", "hst")),
    )
    out_specs = (P(("req", "hst"), None), P(("req", "hst"), None))
    return jax.shard_map(body, mesh=mesh, in_specs=in_specs, out_specs=out_specs, check_vma=False)
```

profile of v0, /device:TPU:1, one launch (start us, length us, event | category | flops | bytes accessed | tf_op | source)
XLA Modules:
  0.0 220.3 jit_solution(2751996907084913244)
XLA Ops:
  7.8 23.9 %all-gather = bf16[16,2,4096]{2,1,0:T(2,128)(2,1)S(1)} all-gather(bf16[1,2,4096]{2,1,0:T(2,128)(2,1)} %bitcast.83), channel_id=1, replica_groups=mesh['req'=2,'hst'=16] {'hst'}, dimensions={0}, use_global_device_ids=true | all-gather | bytes 278528 | tf_op jit(solution)/shard_map/all_gather | solution.py:76
  31.9 17.8 %all-gather.1 = bf16[16,2,512]{2,1,0:T(2,128)(2,1)S(1)} all-gather(bf16[1,2,512]{2,1,0:T(2,128)(2,1)} %bitcast.84), channel_id=1, replica_groups=mesh['req'=2,'hst'=16] {'hst'}, dimensions={0}, use_global_device_ids=true | all-gather | bytes 34816 | tf_op jit(solution)/shard_map/all_gather | solution.py:77
  49.7 19.1 %all-gather.2 = bf16[16,2,512]{2,1,0:T(2,128)(2,1)S(1)} all-gather(bf16[1,2,512]{2,1,0:T(2,128)(2,1)} %bitcast.85), channel_id=1, replica_groups=mesh['req'=2,'hst'=16] {'hst'}, dimensions={0}, use_global_device_ids=true | all-gather | bytes 34816 | tf_op jit(solution)/shard_map/all_gather | solution.py:78
  71.9 14.5 %while.33 = (s32[]{:T(128)}, f32[32,32]{1,0:T(8,128)}, f32[32,32]{1,0:T(8,128)}, f32[32,4096]{1,0:T(8,128)S(1)}, pred[32,160]{1,0:T(8,128)(4,1)S(1)}, /*index=5*...) while((s32[]{:T(128)}, f32[32,32]{1,0:T(8,128)}, ...), condition=%wide.region_9.10_spmd, body=%wide.region_6.9_spmd.sunk | while | flops 21257740 | bytes 1424703 | solution.py:52
  72.3 1.3 dynamic_update_slice.46
  73.8 1.3 dynamic_update_slice.47
  75.8 1.4 dynamic_update_slice.46
  77.4 1.4 dynamic_update_slice.47
  79.5 1.4 dynamic_update_slice.46
  81.1 1.4 dynamic_update_slice.47
  83.1 1.4 dynamic_update_slice.46
  84.8 1.4 dynamic_update_slice.47
  86.5 3.5 %all-to-all-start.1 = ((f32[1,32,32]{2,0,1:T(1,128)}), f32[1,32,32]{2,0,1:T(1,128)S(1)}, u32[]{:S(2)}, u32[]{:S(2)}) async-start(f32[1,32,32]{2,0,1:T(1,128)} %bitcast.10), calls=%async_computation.1 | async-start | bytes 32768 | tf_op jit(solution)/shard_map/all_to_all | solution.py:94
  91.0 4.9 %all-to-all-done.1 = f32[1,32,32]{2,0,1:T(1,128)S(1)} async-done(((f32[1,32,32]{2,0,1:T(1,128)}), f32[1,32,32]{2,0,1:T(1,128)S(1)}, u32[]{:S(2)}, u32[]{:S(2)}) %all-to-all-start.1) | async-done | bytes 4128 | tf_op jit(solution)/shard_map/all_to_all | solution.py:94
  95.8 4.0 %all-to-all-start.2 = ((f32[1,32,32]{2,0,1:T(1,128)}), f32[1,32,32]{2,0,1:T(1,128)S(1)}, u32[]{:S(2)}, u32[]{:S(2)}) async-start(f32[1,32,32]{2,0,1:T(1,128)} %bitcast.12), calls=%async_computation.2 | async-start | bytes 32768 | tf_op jit(solution)/shard_map/all_to_all | solution.py:95
  99.9 1.4 broadcast_in_dim.110
  101.3 4.5 %all-to-all-done.2 = f32[1,32,32]{2,0,1:T(1,128)S(1)} async-done(((f32[1,32,32]{2,0,1:T(1,128)}), f32[1,32,32]{2,0,1:T(1,128)S(1)}, u32[]{:S(2)}, u32[]{:S(2)}) %all-to-all-start.2) | async-done | bytes 4128 | tf_op jit(solution)/shard_map/all_to_all | solution.py:95
  105.8 4.2 %all-to-all-start = ((f32[1,32,4096]{2,0,1:T(1,128)}), f32[1,32,4096]{2,0,1:T(1,128)S(1)}, u32[]{:S(2)}, u32[]{:S(2)}) async-start(f32[1,32,4096]{2,0,1:T(1,128)} %broadcast_in_dim.110), calls=%async_computation | async-start | bytes 1048576 | tf_op jit(solution)/shard_map/all_to_all | solution.py:96
  110.6 78.9 %all-reduce.4.cloned.1.call-done = (bf16[128,512]{0,1:T(8,128)(2,1)}, bf16[128,512]{0,1:T(8,128)(2,1)}) async-done(((bf16[128,512]{0,1:T(8,128)(2,1)}, bf16[128,512]{0,1:T(8,128)(2,1)}), (bf16[128,512]{0,1:T(8,128)(2,1)}, bf16[128,512]{0,1:T(8,128)(2,1)})) %all-reduce.4.cloned.1.call-update) | async-done | bytes 262160 | tf_op jit(solution)/shard_map/psum | solution.py:15
  191.4 1.6 broadcast_in_dim.107.clone2
  193.0 13.8 %while.32 = (s32[]{:T(128)}, f32[128,32]{0,1:T(8,128)S(1)}, f32[128,4096]{1,0:T(8,128)}, pred[128,256]{1,0:T(8,128)(4,1)S(1)}, bf16[128,4096]{1,0:T(8,128)(2,1)}...) while((s32[]{:T(128)}, f32[128,32]{0,1:T(8,128)S(1)}, ...), condition=%wide.region_5.6_spmd, body=%wide.region_2.5_spmd.sunk | while | flops 136050688 | bytes 7266611 | solution.py:52
  193.0 1.0 constant_dynamic-slice_fusion.2
  208.3 2.6 %fusion.25 = bf16[128,4096]{1,0:T(8,128)(2,1)} fusion(f32[128,4096]{1,0:T(8,128)S(1)} %copy-done, f32[16,8,32,128]{3,2,1,0:T(8,128)S(1)} %bitcast.78, pred[128]{0:T(512)(128)(4,1)S(1)} %iota_compare_fusion.2), kind=kLoop, calls=%fused_computation.33 | loop fusion | flops 1572864 | bytes 5243008 | tf_op jit(solution)/shard_map/convert_element_type | solution.py:74
  210.9 1.2 reduce
  (96 shorter events, 25.2 us)
Async XLA Ops:
  71.9 18.1 %copy-start.1 = (bf16[128,512]{1,0:T(8,128)(2,1)S(1)}, bf16[128,512]{1,0:T(8,128)(2,1)}, u32[]{:S(2)}) copy-start(bf16[128,512]{1,0:T(8,128)(2,1)} %param.12) | copy-start | bytes 393220
  71.9 18.2 %copy-start.2 = (bf16[128,512]{1,0:T(8,128)(2,1)S(1)}, bf16[128,512]{1,0:T(8,128)(2,1)}, u32[]{:S(2)}) copy-start(bf16[128,512]{1,0:T(8,128)(2,1)} %param.13) | copy-start | bytes 393220
  86.5 9.4 %all-to-all-start.1 = ((f32[1,32,32]{2,0,1:T(1,128)}), f32[1,32,32]{2,0,1:T(1,128)S(1)}, u32[]{:S(2)}, u32[]{:S(2)}) async-start(f32[1,32,32]{2,0,1:T(1,128)} %bitcast.10), calls=%async_computation.1 | async-start | bytes 32768 | tf_op jit(solution)/shard_map/all_to_all | solution.py:94
  89.9 99.6 %all-reduce.4.cloned.1.call-start = ((), (), s32[]{:S(2)}) async-start(), calls=%async_computation.3 | async-start | bytes 524288 | tf_op jit(solution)/shard_map/psum | solution.py:15
  95.8 10.0 %all-to-all-start.2 = ((f32[1,32,32]{2,0,1:T(1,128)}), f32[1,32,32]{2,0,1:T(1,128)S(1)}, u32[]{:S(2)}, u32[]{:S(2)}) async-start(f32[1,32,32]{2,0,1:T(1,128)} %bitcast.12), calls=%async_computation.2 | async-start | bytes 32768 | tf_op jit(solution)/shard_map/all_to_all | solution.py:95
  105.8 105.1 %all-to-all-start = ((f32[1,32,4096]{2,0,1:T(1,128)}), f32[1,32,4096]{2,0,1:T(1,128)S(1)}, u32[]{:S(2)}, u32[]{:S(2)}) async-start(f32[1,32,4096]{2,0,1:T(1,128)} %broadcast_in_dim.110), calls=%async_computation | async-start | bytes 1048576 | tf_op jit(solution)/shard_map/all_to_all | solution.py:96
  206.7 1.6 copy-start
Sparse Core Ops, SparseCore 0:
  94.8 94.6 all-reduce.3
where the time goes:
time: 221 us; the launch traced here: 220 us
  waiting for transfers between devices  88.3 us (40%)
  blocking collectives  60.8 us (28%)
  local copies, waits for them, and re-layouts  27.2 us (12%)
  between operations  14.9 us (7%)
  starting transfers between devices  11.7 us (5%)
  other arithmetic  11.6 us (5%)
  matrix products  5.35 us (2%)
    psum x1, waiting for transfers between devices, from_root(): return lax.psum(jnp.where(mine, array, jnp.zeros_like(array)), axis)  78.9 us
    all_gather x1, blocking collectives, body(): lax.all_gather(ask_q, 'hst', axis=0, tiled=True)  23.9 us
    all_gather x1, blocking collectives, body(): lax.all_gather(ask_v, 'hst', axis=0, tiled=True)  19.1 us
    all_gather x1, blocking collectives, body(): lax.all_gather(ask_k, 'hst', axis=0, tiled=True)  17.8 us
    dynamic_update_slice x8, local copies, waits for them, and re-layouts, one_group(): lax.dynamic_update_slice_in_dim(totals, row_sum, group_index * group_size...  5.62 us
    dynamic_update_slice x4, local copies, waits for them, and re-layouts, one_group(): lax.dynamic_update_slice_in_dim(maxima, row_max, group_index * group_size...  5.61 us
    all_to_all x1, waiting for transfers between devices, body(): lax.all_to_all(ask_max[None], 'hst', split_axis=1, concat_axis=0, tiled=T...  4.86 us
    dynamic_slice x8, local copies, waits for them, and re-layouts, one_group(): lax.dynamic_slice_in_dim(queries, group_index * group_width, group_width, 1)  4.54 us
  transfers between devices with their start and end apart: 4, of which 3 were waited for; matrix products, arithmetic and copies ran while one was open for 11% of the time, Pallas kernels for 0%

commit v1 on v0

v1 whole, which is shorter than its diff:
```python
import functools
import math

import jax
import jax.numpy as jnp
from jax import lax
from jax.experimental import pallas as pl
from jax.experimental.pallas import tpu as pltpu
from jax.sharding import PartitionSpec as P

H = 32
KVH = 4
DH = 128
HEADS = H // KVH
SUB = 16
SCALE = 1.0 / math.sqrt(DH)
NEG = -math.inf
COSTS = {'ask': 20000000000.0, 'merge': 20000000000.0, 'regroup': 10000000000.0, 'gate': 20000000000.0}
BF16 = jnp.bfloat16
F32 = jnp.float32
VMEM = pl.BlockSpec(memory_space=pltpu.VMEM)
SMEM = pl.BlockSpec(memory_space=pltpu.SMEM)
HBM = pl.BlockSpec(memory_space=pltpu.HBM)


def round_up(value, step):
    return -(-value // step) * step


def params(**more):
    return pltpu.CompilerParams(vmem_limit_bytes=32 * 2**20, **more)


def dot_nt(a, b):
    return lax.dot_general(a, b, (((1,), (1,)), ((), ())), preferred_element_type=F32)


def dot_nn(a, b):
    return lax.dot_general(a, b, (((1,), (0,)), ((), ())), preferred_element_type=F32)


def head_columns(head, width=DH):
    return pl.ds(pl.multiple_of(head * width, width), width)


def diagonal(rows):
    shape = (rows, DH)
    return lax.broadcasted_iota(jnp.int32, shape, 0) == lax.broadcasted_iota(jnp.int32, shape, 1)


def place():
    return lax.rem(lax.axis_index("hst"), KVH)


def gate_kernel(mark_ref):
    mark_ref[...] = jnp.zeros(mark_ref.shape, F32)


def pack_kernel(valid_ref, q_ref, ak_ref, av_ref, k_ref, v_ref, earlier_ref, *refs):
    del earlier_ref
    q_outs, kv_outs = refs[:KVH], refs[KVH:]
    tokens = q_ref.shape[0]
    block = k_ref.shape[0]
    me = place()
    count = jnp.full((1, DH), valid_ref[0], jnp.int32).astype(F32)
    for x in range(KVH):
        head = jnp.bitwise_xor(me, x)
        q = q_ref[:, head_columns(head, HEADS * DH)].astype(F32)
        rows = [q[t : t + 1, h * DH : (h + 1) * DH] for t in range(tokens) for h in range(HEADS)]
        rows.append(ak_ref[:, head_columns(head)].astype(F32))
        rows.append(av_ref[:, head_columns(head)].astype(F32))
        rows.append(count)
        spare = q_outs[x].shape[0] - tokens * HEADS - 2 * tokens - 1
        if spare:
            rows.append(jnp.zeros((spare, DH), F32))
        q_outs[x][...] = jnp.concatenate(rows, axis=0).astype(BF16)
    for x in range(KVH):
        cols = head_columns(jnp.bitwise_xor(me, x))
        kv_outs[x][:block, :] = k_ref[:, cols]
        kv_outs[x][block:, :] = v_ref[:, cols]


def regroup_kernel(tokens, *refs):
    pieces, out_ref = refs[:KVH], refs[-1]
    rows_q = tokens * HEADS
    extra = []
    for x in range(KVH):
        out_ref[x * rows_q : (x + 1) * rows_q, :] = pieces[x][:rows_q, :]
        extra.append(pieces[x][rows_q:, :].astype(F32)[: 2 * tokens, :])
    out_ref[KVH * rows_q :, :] = jnp.concatenate(extra, axis=0).astype(BF16)


def ask_kernel(hosts, tokens, *refs):
    groups = hosts // KVH
    z_refs, q_refs, kv_refs = refs[:groups], refs[groups : groups + KVH], refs[groups + KVH :]
    kv_refs, out_ref = kv_refs[:KVH], kv_refs[KVH]
    rows_q = tokens * HEADS
    rows_z = KVH * rows_q
    me = place()
    group = lax.axis_index("hst") // KVH
    last_group = group == groups - 1
    block = kv_refs[0].shape[0] // 2
    total_rows = groups * rows_z
    q = jnp.concatenate([z[:rows_z, :] for z in z_refs], axis=0)
    extra = jnp.concatenate([z[rows_z:, :] for z in z_refs], axis=0)
    asks = hosts * tokens

    def token_of(index, per_group, per_host, per_token):
        from_group = jnp.bitwise_xor(index // per_group, group)
        from_place = jnp.bitwise_xor(index % per_group // per_host, me)
        return (from_group * KVH + from_place) * tokens + index % per_host // per_token

    per_host = 2 * tokens
    wide = groups * KVH * per_host
    u = lax.broadcasted_iota(jnp.int32, (asks, wide), 0)
    c = lax.broadcasted_iota(jnp.int32, (1, wide), 1)
    part = c % per_host
    token = token_of(c - part + part % tokens, KVH * per_host, per_host, 1)
    token_k = jnp.where(part < tokens, token, -1)
    token_v = jnp.where(part < tokens, -1, token)
    ask_k = dot_nn(jnp.where(u == token_k, 1.0, 0.0).astype(BF16), extra).astype(BF16)
    ask_v = dot_nn(jnp.where(u == token_v, 1.0, 0.0).astype(BF16), extra).astype(BF16)

    row = lax.broadcasted_iota(jnp.int32, (total_rows, 1), 0)
    row_token = token_of(row, rows_z, rows_q, HEADS)
    col = lax.broadcasted_iota(jnp.int32, (total_rows, asks), 1)
    s = dot_nt(q, ask_k) * SCALE
    ask_scores = jnp.where((col <= row_token) & last_group, s, NEG)
    ask_best = jnp.max(ask_scores, axis=1, keepdims=True)
    ask_shift = ask_best
    lane = lax.broadcasted_iota(jnp.int32, (1, block), 1).astype(F32)
    tops, sums, mixes = [], [], []
    for x in range(KVH):
        s = dot_nt(q, kv_refs[x][:block, :]) * SCALE
        is_last = last_group & (jnp.bitwise_xor(me, x) == KVH - 1)
        info = q_refs[x][rows_q:, :].astype(F32)
        count = info[2 * tokens : 2 * tokens + 1, :1]
        s = jnp.where(lane < count, s, NEG)
        top = jnp.max(s, axis=1, keepdims=True)
        top = jnp.where(is_last, jnp.maximum(top, ask_best), top)
        ask_shift = jnp.where(is_last, top, ask_shift)
        e = jnp.exp(s - top)
        tops.append(top)
        sums.append(jnp.sum(e, axis=1, keepdims=True))
        mixes.append(dot_nn(e.astype(BF16), kv_refs[x][block:, :]))
    ask_shift = jnp.where(last_group, ask_shift, 0.0)
    e = jnp.exp(ask_scores - ask_shift)
    sums.append(jnp.sum(e, axis=1, keepdims=True))
    mixes.append(dot_nn(e.astype(BF16), ask_v))
    best = functools.reduce(jnp.maximum, tops).astype(BF16).astype(F32)
    factors = [jnp.exp(top - best) for top in tops]
    factors.append(jnp.where(last_group, jnp.exp(ask_shift - best), 0.0))
    total = functools.reduce(jnp.add, [f * part for f, part in zip(factors, sums)])
    mixed = functools.reduce(jnp.add, [f * part for f, part in zip(factors, mixes)])
    mask = diagonal(rows_q)
    total_high = total.astype(BF16).astype(F32)
    mixed_high = mixed.astype(BF16).astype(F32)
    stats = (best, total_high, total - total_high)
    spare = jnp.zeros((out_ref.shape[1] - 2 * rows_q - len(stats), DH), F32)
    for d in range(groups):
        for x in range(KVH):
            at = d * rows_z + x * rows_q
            rows = slice(at, at + rows_q)
            to = jnp.bitwise_xor(group, d) * KVH + jnp.bitwise_xor(me, x)
            pieces = [mixed_high[rows], mixed[rows] - mixed_high[rows]]
            for stat in stats:
                pieces.append(jnp.sum(jnp.where(mask, stat[rows], 0.0), axis=0, keepdims=True))
            out_ref[to] = jnp.concatenate([*pieces, spare], axis=0).astype(BF16)


def merge_kernel(recv_ref, out_ref):
    tokens = out_ref.shape[0]
    rows_q = tokens * HEADS
    groups = recv_ref.shape[0] // KVH
    mask = diagonal(rows_q)
    lines = [[] for _ in range(tokens)]
    for g in range(KVH):
        parts = [recv_ref[j * KVH + g].astype(F32) for j in range(groups)]

        tops = [part[2 * rows_q : 2 * rows_q + 1, :] for part in parts]
        best = functools.reduce(jnp.maximum, tops)
        factors = [jnp.exp(top - best) for top in tops]
        total = jnp.zeros((1, DH), F32)
        for f, part in zip(factors, parts):
            high, low = (part[2 * rows_q + i : 2 * rows_q + i + 1, :] for i in (1, 2))
            total = total + f * (high + low)
        scale = 1.0 / total
        normed = jnp.zeros((rows_q, DH), F32)
        for f, part in zip(factors, parts):
            weight = jnp.sum(jnp.where(mask, f * scale, 0.0), axis=1, keepdims=True)
            normed = normed + weight * (part[:rows_q, :] + part[rows_q : 2 * rows_q, :])
        for t in range(tokens):
            for h in range(HEADS):
                lines[t].append(normed[t * HEADS + h : t * HEADS + h + 1, :])
    rows = [jnp.concatenate(line, axis=1) for line in lines]
    out_ref[...] = jnp.concatenate(rows, axis=0).astype(BF16)


def ctx_kernel(xs, before, valid_ref, q_ref, k_ref, v_ref, *refs):
    anchors, refs = refs[: len(xs)], refs[len(xs) :]
    if before:
        _, out_hbm, bias_ref, keep_ref, out_ref, sems = refs
    else:
        out_hbm, mark_ref, bias_ref, keep_ref, out_ref, sems = refs
        mark_ref[...] = jnp.zeros(mark_ref.shape, F32)
    block = k_ref.shape[0]
    host = lax.axis_index("hst")
    me = lax.rem(host, KVH)
    count = valid_ref[0]
    row = lax.broadcasted_iota(jnp.int32, (block, block), 0)
    col = lax.broadcasted_iota(jnp.int32, (block, block), 1)
    bias_ref[:, :block] = jnp.broadcast_to(jnp.where(host > 0, 0.0, NEG), (block, block))
    bias_ref[:, block:] = jnp.where((col <= row) & (col < count), 0.0, NEG)
    keep_ref[...] = jnp.where(lax.broadcasted_iota(jnp.int32, (block, DH), 0) < count, 1.0, 0.0)
    wide = HEADS // 4 * DH
    copies = []
    for i, x in enumerate(xs):
        head = jnp.bitwise_xor(me, x)
        cols = head_columns(head)
        keys = jnp.concatenate([anchors[i][:block, :], k_ref[:, cols]], axis=0)
        values = jnp.concatenate([anchors[i][block:, :], v_ref[:, cols]], axis=0)
        for h in range(HEADS):
            at = pl.ds(pl.multiple_of(head * (HEADS * DH) + h * DH, DH), DH)
            s = dot_nt(q_ref[:, at], keys) * SCALE + bias_ref[...]
            best = jnp.max(s, axis=1, keepdims=True)
            e = jnp.exp(s - best)
            total = jnp.sum(e, axis=1, keepdims=True)
            mixed = dot_nn(e.astype(BF16), values)
            out_ref[i, :, h * DH : (h + 1) * DH] = (
                mixed * (keep_ref[...] * (1.0 / total))
            ).astype(BF16)
            if (h + 1) * DH % wide == 0:
                part = (h + 1) * DH // wide - 1
                to = pl.ds(pl.multiple_of(head * (HEADS * DH) + part * wide, wide), wide)
                copy = pltpu.make_async_copy(
                    out_ref.at[i, :, part * wide : (part + 1) * wide],
                    out_hbm.at[:, to],
                    sems.at[i, part],
                )
                copy.start()
                copies.append(copy)
    for copy in copies:
        copy.wait()


def ctx_call(valid, q, k, v, pieces, before=()):
    block, width = q.shape
    xs, anchors = zip(*pieces)
    operands = [valid, q, k, v, *anchors, *before]
    outs, specs = [jax.ShapeDtypeStruct(q.shape, BF16)], [HBM]
    if not before:
        outs, specs = outs + [jax.ShapeDtypeStruct((8, DH), F32)], specs + [VMEM]
    return pl.pallas_call(
        functools.partial(ctx_kernel, xs, bool(before)),
        out_shape=outs,
        in_specs=[SMEM] + [VMEM] * (3 + len(xs)) + [HBM] * len(before),
        out_specs=specs,
        scratch_shapes=[
            pltpu.VMEM((block, 2 * block), F32),
            pltpu.VMEM((block, DH), F32),
            pltpu.VMEM((len(xs), block, HEADS * DH), BF16),
            pltpu.SemaphoreType.DMA((len(xs), 4)),
        ],
        input_output_aliases={len(operands) - 1: 0} if before else {},
        compiler_params=params(),
        cost_estimate=pl.CostEstimate(flops=int(COSTS.get("ctx", 1)), bytes_accessed=1, transcendentals=0),
        name="ctx",
    )(*operands)


def after_kernel(in_ref, mark_ref, out_ref):
    del mark_ref
    out_ref[...] = in_ref[...]


def small_call(kernel, outs, ins, operands, name, scratch=(), mib=32, out_space=VMEM):
    return pl.pallas_call(
        kernel,
        out_shape=outs,
        in_specs=ins,
        out_specs=jax.tree.map(lambda _: out_space, outs),
        scratch_shapes=scratch,
        compiler_params=pltpu.CompilerParams(vmem_limit_bytes=mib * 2**20),
        cost_estimate=pl.CostEstimate(flops=int(COSTS.get(name, 1)), bytes_accessed=1, transcendentals=0),
        name=name,
    )(*operands)


def body(hosts, ctx_q, ctx_k, ctx_v, ask_q, ask_k, ask_v, valid):
    block = ctx_q.shape[0]
    tokens = ask_q.shape[0]
    groups = hosts // KVH
    rows_q = tokens * HEADS
    rows_all = KVH * (rows_q + 2 * tokens)
    shape = jax.ShapeDtypeStruct
    me = place()
    group = lax.axis_index("hst") // KVH

    def near(array, x):
        return lax.ppermute(array, "hst", [(i, i ^ x) for i in range(hosts)])

    def far(array, d):
        return lax.ppermute(array, "hst", [(i, i ^ (d * KVH)) for i in range(hosts)])

    def from_first(array, d):
        order = [0, *range(d, groups), *range(d - 1, 0, -1)]
        after = dict(zip(order, order[1:] + order[:1]))
        if d == 1:
            after = {a: a ^ 1 for a in range(groups)}
        return lax.ppermute(
            array, "hst", [(i, after[i // KVH] * KVH + i % KVH) for i in range(hosts)]
        )

    mark = small_call(gate_kernel, shape((8, DH), F32), [], (), "gate")
    packed = small_call(
        pack_kernel,
        [shape((rows_q + round_up(2 * tokens + 1, SUB), DH), BF16)] * KVH
        + [shape((2 * block, DH), BF16)] * KVH,
        [SMEM] + [VMEM] * 6,
        (valid, ask_q, ask_k, ask_v, ctx_k, ctx_v, mark),
        "pack",
    )
    qs = [packed[0]] + [near(packed[x], x) for x in range(1, KVH)]
    kvs = [packed[KVH]] + [near(packed[KVH + x], x) for x in range(1, KVH)]
    mine = small_call(
        functools.partial(regroup_kernel, tokens), shape((rows_all, DH), BF16), [VMEM] * KVH, qs, "regroup"
    )
    again = small_call(
        after_kernel, shape(mine.shape, BF16), [VMEM] * 2, (mine, kvs[1]), "again"
    )
    zs = [mine, far(again, 1)] + [far(mine, d) for d in range(2, groups)]

    anchor = kvs[0]
    for x in range(1, KVH):
        anchor = jnp.where(me == x, kvs[x], anchor)
    arrived = [from_first(anchor, d) for d in range(1, groups)]
    for d in range(1, groups):
        anchor = jnp.where(group == d, arrived[d - 1], anchor)
    parts = small_call(
        functools.partial(ask_kernel, hosts, tokens),
        shape((hosts, 2 * rows_q + 8, DH), BF16),
        [VMEM] * (groups + 2 * KVH),
        (*zs, *qs, *kvs),
        "ask",
    )
    parts = lax.all_to_all(parts, "hst", split_axis=0, concat_axis=0, tiled=True)
    half = KVH // 2
    context = functools.partial(ctx_call, valid, ctx_q, ctx_k, ctx_v)
    ctx_out, mark = context([(0, anchor)] + [(x, near(anchor, x)) for x in range(1, half)])
    second = small_call(
        after_kernel, shape(anchor.shape, BF16), [VMEM] * 2, (near(anchor, half), mark), "after"
    )
    pieces = [(half, second)] + [(half + x, near(second, x)) for x in range(1, half)]
    (ctx_out,) = context(pieces, (ctx_out,))
    ask_out = small_call(merge_kernel, shape(ask_q.shape, BF16), [VMEM], (parts,), "merge")
    return (ctx_out, ask_out)


def solution(mesh):
    rows = P(("req", "hst"), None)
    return jax.shard_map(
        functools.partial(body, mesh.shape["hst"]),
        mesh=mesh,
        in_specs=(rows,) * 6 + (P(("req", "hst")),),
        out_specs=(rows, rows),
        check_vma=False,
    )
```

time: 221 us -> 32.1 us (0.15)
  waiting for transfers between devices: 88.3 us -> 3.09 us
  blocking collectives: 60.8 us -> 0 us
  local copies, waits for them, and re-layouts: 27.2 us -> 0.21 us
  between operations: 14.9 us -> 1.49 us
  other arithmetic: 11.6 us -> 0.03 us
  starting transfers between devices: 11.7 us -> 20.6 us
  Pallas kernels: 0 us -> 6.12 us
  matrix products: 5.35 us -> 0 us
    psum x1 -> x0, waiting for transfers between devices: 78.9 us -> none  [from_root(): return lax.psum(jnp.where(mine, array, jnp.zeros_like(array)), axis)]
    all_gather x3 -> x0, blocking collectives: 60.8 us -> none  [the longest x1 23.9 us: body(): lax.all_gather(ask_q, 'hst', axis=0, tiled=True)]
    ppermute x0 -> x15, starting transfers between devices: none -> 15.8 us  [the longest x9 8.05 us: near(): return lax.ppermute(array, 'hst', [(i, i ^ x) for i in range(hosts)])]
    dynamic_update_slice x24 -> x0, local copies, waits for them, and re-layouts: 15.5 us -> none  [the longest x8 5.62 us: one_group(): lax.dynamic_update_slice_in_dim(totals, row_sum, group_index * group_size...]
    all_to_all x3 -> x1, waiting for transfers between devices: 9.35 us -> 0.01 us  [body(): lax.all_to_all(parts, 'hst', split_axis=0, concat_axis=0, tiled=True)]
    all_to_all x3 -> x1, starting transfers between devices: 11.7 us -> 4.83 us  [body(): lax.all_to_all(parts, 'hst', split_axis=0, concat_axis=0, tiled=True)]
    pallas_call x0 -> x9, Pallas kernels: none -> 6.12 us  [the longest x2 3.81 us: ctx_call(): pl.pallas_call(functools.partial(ctx_kernel, xs, bool(before)), out_shape...]
    dot_general x16 -> x0, matrix products: 5.35 us -> none  [the longest x8 2.9 us: one_group(): jnp.einsum('rgd,sd->rgs', query_part, key_part, preferred_element_type=jn...]
  transfers between devices with their start and end apart: 4 -> 16, of which waited for: 3 -> 3; matrix products, arithmetic and copies ran while one was open for 11% -> 0% of each run, Pallas kernels for 0% -> 17%
where the time goes in v1:
time: 32.1 us; the launch traced here: 31.5 us
  starting transfers between devices  20.6 us (64%)
  Pallas kernels  6.12 us (19%)
  waiting for transfers between devices  3.09 us (10%)
  between operations  1.49 us (5%)
    ppermute x9, starting transfers between devices, near(): return lax.ppermute(array, 'hst', [(i, i ^ x) for i in range(hosts)])  8.05 us
    all_to_all x1, starting transfers between devices, body(): lax.all_to_all(parts, 'hst', split_axis=0, concat_axis=0, tiled=True)  4.83 us
    ppermute x3, starting transfers between devices, from_first(): lax.ppermute(array, 'hst', [(i, after[i // KVH] * KVH + i % KVH) for i in...  4 us
    pallas_call x2, Pallas kernels, ctx_call(): pl.pallas_call(functools.partial(ctx_kernel, xs, bool(before)), out_shape...  3.81 us
    ppermute x3, starting transfers between devices, far(): return lax.ppermute(array, 'hst', [(i, i ^ d * KVH) for i in range(hosts)])  3.71 us
    ppermute x9, waiting for transfers between devices, near(): return lax.ppermute(array, 'hst', [(i, i ^ x) for i in range(hosts)])  3.08 us
    pallas_call x7, Pallas kernels, small_call(): pl.pallas_call(kernel, out_shape=outs, in_specs=ins, out_specs=jax.tree.m...  2.32 us
  transfers between devices with their start and end apart: 16, of which 3 were waited for; matrix products, arithmetic and copies ran while one was open for 0% of the time, Pallas kernels for 17%

profile of v1, /device:TPU:1, one launch (start us, length us, event | category | flops | bytes accessed | tf_op | source)
XLA Modules:
  0.0 31.5 jit_solution(17378057384558334514)
XLA Ops:
  1.4 0.1 copy-done.2
  1.5 0.1 copy-done.1
  1.6 0.1 pack.1
  1.7 0.1 collective-permute-start.9
  1.8 2.7 %collective-permute-start.10 = (bf16[32,128]{1,0:T(8,128)(2,1)S(1)}, bf16[32,128]{1,0:T(8,128)(2,1)S(1)}, u32[]{:S(2)}, u32[]{:S(2)}) collective-permute-start(bf16[32,128]{1,0:T(8,128)(2,1)S(1)} %get-tuple-element.20), channel_id=1, source_target_pairs={{0,2},{1,3},{2,0},{3,1},{4,6},{5,7},{6,4},{7,5},{8,10},{9,11},{10,... | collective-permute-start | bytes 24584 | tf_op jit(solution)/shard_map/ppermute | solution.py:300
  4.5 0.0 collective-permute-start.11
  4.6 1.7 %collective-permute-start = (bf16[256,128]{1,0:T(8,128)(2,1)S(1)}, bf16[256,128]{1,0:T(8,128)(2,1)S(1)}, u32[]{:S(2)}, u32[]{:S(2)}) collective-permute-start(bf16[256,128]{1,0:T(8,128)(2,1)S(1)} %get-tuple-element.12), channel_id=1, source_target_pairs={{0,3},{1,2},{2,1},{3,0},{4,7},{5,6},{6,5},{7,4},{8,11},{9,10},{10,... | collective-permute-start | bytes 196616 | tf_op jit(solution)/shard_map/ppermute | solution.py:300
  6.3 0.4 %collective-permute-start.2 = (bf16[256,128]{1,0:T(8,128)(2,1)S(1)}, bf16[256,128]{1,0:T(8,128)(2,1)S(1)}, u32[]{:S(2)}, u32[]{:S(2)}) collective-permute-start(bf16[256,128]{1,0:T(8,128)(2,1)S(1)} %get-tuple-element.14), channel_id=1, source_target_pairs={{0,1},{1,0},{2,3},{3,2},{4,5},{5,4},{6,7},{7,6},{8,9},{9,8},{10,11... | collective-permute-start | bytes 196616 | tf_op jit(solution)/shard_map/ppermute | solution.py:300
  6.7 1.2 %collective-permute-done.11.refs_3_.refs_7_ = bf16[32,128]{1,0:T(8,128)(2,1)S(1)} collective-permute-done((bf16[32,128]{1,0:T(8,128)(2,1)S(1)}, bf16[32,128]{1,0:T(8,128)(2,1)S(1)}, u32[]{:S(2)}, u32[]{:S(2)}) %collective-permute-start.11) | collective-permute-done | bytes 8224 | tf_op jit(solution)/shard_map/ppermute | solution.py:300
  8.0 3.3 %collective-permute-start.14 = (bf16[80,128]{1,0:T(8,128)(2,1)S(1)}, bf16[80,128]{1,0:T(8,128)(2,1)S(1)}, u32[]{:S(2)}, u32[]{:S(2)}) collective-permute-start(bf16[80,128]{1,0:T(8,128)(2,1)S(1)} %regroup.1.in_ref.refs_0_), channel_id=1, source_target_pairs={{0,12},{1,13},{2,14},{3,15},{4,8},{5,9},{6,10},{7,11},{8,4},{9,5},... | collective-permute-start | bytes 61448 | tf_op jit(solution)/shard_map/ppermute | solution.py:303
  11.3 0.4 %collective-permute-start.12 = (bf16[80,128]{1,0:T(8,128)(2,1)S(1)}, bf16[80,128]{1,0:T(8,128)(2,1)S(1)}, u32[]{:S(2)}, u32[]{:S(2)}) collective-permute-start(bf16[80,128]{1,0:T(8,128)(2,1)S(1)} %again.1), channel_id=1, source_target_pairs={{0,4},{1,5},{2,6},{3,7},{4,0},{5,1},{6,2},{7,3},{8,12},{9,13},{10,... | collective-permute-start | bytes 61448 | tf_op jit(solution)/shard_map/ppermute | solution.py:303
  11.7 1.2 %collective-permute-start.5 = (bf16[256,128]{1,0:T(8,128)(2,1)S(1)}, bf16[256,128]{1,0:T(8,128)(2,1)S(1)}, u32[]{:S(2)}, u32[]{:S(2)}) collective-permute-start(bf16[256,128]{1,0:T(8,128)(2,1)S(1)} %select_select_fusion.1), channel_id=1, source_target_pairs={{0,4},{1,5},{2,6},{3,7},{4,0},{5,1},{6,2},{7,3},{8,12},{9,13},{10,... | collective-permute-start | bytes 196616 | tf_op jit(solution)/shard_map/ppermute | solution.py:310
  12.9 2.3 %collective-permute-start.4 = (bf16[256,128]{1,0:T(8,128)(2,1)S(1)}, bf16[256,128]{1,0:T(8,128)(2,1)S(1)}, u32[]{:S(2)}, u32[]{:S(2)}) collective-permute-start(bf16[256,128]{1,0:T(8,128)(2,1)S(1)} %select_select_fusion.1), channel_id=1, source_target_pairs={{0,8},{1,9},{2,10},{3,11},{4,0},{5,1},{6,2},{7,3},{8,12},{9,13},{1... | collective-permute-start | bytes 196616 | tf_op jit(solution)/shard_map/ppermute | solution.py:310
  15.2 0.5 %collective-permute-start.3 = (bf16[256,128]{1,0:T(8,128)(2,1)S(1)}, bf16[256,128]{1,0:T(8,128)(2,1)S(1)}, u32[]{:S(2)}, u32[]{:S(2)}) collective-permute-start(bf16[256,128]{1,0:T(8,128)(2,1)S(1)} %select_select_fusion.1), channel_id=1, source_target_pairs={{0,12},{1,13},{2,14},{3,15},{4,0},{5,1},{6,2},{7,3},{8,4},{9,5},{1... | collective-permute-start | bytes 196616 | tf_op jit(solution)/shard_map/ppermute | solution.py:310
  15.7 1.5 %ask.1 = bf16[16,40,128]{2,1,0:T(8,128)(2,1)} custom-call(bf16[80,128]{1,0:T(8,128)(2,1)S(1)} %regroup.1.in_ref.refs_0_, bf16[80,128]{1,0:T(8,128)(2,1)S(1)} %collective-permute-done.12.refs_1_, bf16[80,128]{1,0:T(8,128)(2,1)S(1)} %collective-permute-done.13.refs_2_, bf16[80,128]{1,0:T(8,128)(2,1)S(1)} %collective-permute-done.14.refs_3_, ...), custom_call_target="tpu_custom_call" | custom-call | flops 20000000000 | bytes 1 | tf_op jit(solution)/shard_map/ask/pallas_call | solution.py:277
  17.2 4.8 %all-to-all-start = ((bf16[16,40,128]{2,1,0:T(8,128)(2,1)}), bf16[16,40,128]{2,1,0:T(8,128)(2,1)S(1)}, u32[]{:S(2)}, u32[]{:S(2)}) async-start(bf16[16,40,128]{2,1,0:T(8,128)(2,1)} %ask.1), calls=%async_computation | async-start | bytes 327680 | tf_op jit(solution)/shard_map/all_to_all | solution.py:346
  22.1 0.3 collective-permute-start.7
  22.4 1.5 %collective-permute-start.6 = (bf16[256,128]{1,0:T(8,128)(2,1)S(1)}, bf16[256,128]{1,0:T(8,128)(2,1)S(1)}, u32[]{:S(2)}, u32[]{:S(2)}) collective-permute-start(bf16[256,128]{1,0:T(8,128)(2,1)S(1)} %select_select_fusion.refs_0_), channel_id=1, source_target_pairs={{0,2},{1,3},{2,0},{3,1},{4,6},{5,7},{6,4},{7,5},{8,10},{9,11},{10,... | collective-permute-start | bytes 196616 | tf_op jit(solution)/shard_map/ppermute | solution.py:300
  23.9 1.9 %ctx.2 = (bf16[128,4096]{1,0:T(8,128)(2,1)}, f32[8,128]{1,0:T(8,128)S(1)}) custom-call(s32[1]{0:T(128)S(6)} %copy.11.valid_ref, bf16[128,4096]{1,0:T(8,128)(2,1)S(1)} %copy-done, bf16[128,512]{1,0:T(8,128)(2,1)S(1)} %copy-done.1, bf16[128,512]{1,0:T(8,128)(2,1)S(1)} %copy-done.2, bf16[256,128]{1,0:T(8,128)(2,1)S(1)} %select_select_fusion.refs_0_, ...), custom_call_target="tpu_custom_call" | custom-call | flops 1 | bytes 1 | tf_op jit(solution)/shard_map/ctx/pallas_call | solution.py:253
  25.8 0.9 %collective-permute-done.6.in_ref = bf16[256,128]{1,0:T(8,128)(2,1)S(1)} collective-permute-done((bf16[256,128]{1,0:T(8,128)(2,1)S(1)}, bf16[256,128]{1,0:T(8,128)(2,1)S(1)}, u32[]{:S(2)}, u32[]{:S(2)}) %collective-permute-start.6) | collective-permute-done | bytes 65568 | tf_op jit(solution)/shard_map/ppermute | solution.py:300
  26.7 1.2 %collective-permute-start.8 = (bf16[256,128]{1,0:T(8,128)(2,1)S(1)}, bf16[256,128]{1,0:T(8,128)(2,1)S(1)}, u32[]{:S(2)}, u32[]{:S(2)}) collective-permute-start(bf16[256,128]{1,0:T(8,128)(2,1)S(1)} %after.1.refs_0_), channel_id=1, source_target_pairs={{0,1},{1,0},{2,3},{3,2},{4,5},{5,4},{6,7},{7,6},{8,9},{9,8},{10,11... | collective-permute-start | bytes 196616 | tf_op jit(solution)/shard_map/ppermute | solution.py:300
  27.9 0.9 %collective-permute-done.8.refs_1_ = bf16[256,128]{1,0:T(8,128)(2,1)S(1)} collective-permute-done((bf16[256,128]{1,0:T(8,128)(2,1)S(1)}, bf16[256,128]{1,0:T(8,128)(2,1)S(1)}, u32[]{:S(2)}, u32[]{:S(2)}) %collective-permute-start.8) | collective-permute-done | bytes 65568 | tf_op jit(solution)/shard_map/ppermute | solution.py:300
  28.9 1.9 %ctx.3 = bf16[128,4096]{1,0:T(8,128)(2,1)} custom-call(s32[1]{0:T(128)S(6)} %copy.11.valid_ref, bf16[128,4096]{1,0:T(8,128)(2,1)S(1)} %copy-done, bf16[128,512]{1,0:T(8,128)(2,1)S(1)} %copy-done.1, bf16[128,512]{1,0:T(8,128)(2,1)S(1)} %copy-done.2, bf16[256,128]{1,0:T(8,128)(2,1)S(1)} %after.1.refs_0_, ...), custom_call_target="tpu_custom_call", output_to_operand_aliasing={{}: (6, {})} | custom-call | flops 1 | bytes 1 | tf_op jit(solution)/shard_map/ctx/pallas_call | solution.py:253
  30.8 0.8 %merge.1 = bf16[2,4096]{1,0:T(2,128)(2,1)} custom-call(bf16[16,40,128]{2,1,0:T(8,128)(2,1)S(1)} %all-to-all-done.recv_ref), custom_call_target="tpu_custom_call" | custom-call | flops 20000000000 | bytes 1 | tf_op jit(solution)/shard_map/merge/pallas_call | solution.py:277
  (31 shorter events, 0.1 us)
Async XLA Ops:
  0.6 0.9 %copy-start.2 = (bf16[128,512]{1,0:T(8,128)(2,1)S(1)}, bf16[128,512]{1,0:T(8,128)(2,1)}, u32[]{:S(2)}) copy-start(bf16[128,512]{1,0:T(8,128)(2,1)} %v_ref.5) | copy-start | bytes 393220
  0.6 1.0 %copy-start.1 = (bf16[128,512]{1,0:T(8,128)(2,1)S(1)}, bf16[128,512]{1,0:T(8,128)(2,1)}, u32[]{:S(2)}) copy-start(bf16[128,512]{1,0:T(8,128)(2,1)} %k_ref.5) | copy-start | bytes 393220
  0.7 1.0 %copy-start.3 = (bf16[2,4096]{1,0:T(2,128)(2,1)S(1)}, bf16[2,4096]{1,0:T(2,128)(2,1)}, u32[]{:S(2)}) copy-start(bf16[2,4096]{1,0:T(2,128)(2,1)} %q_ref.3) | copy-start | bytes 49156
  0.7 0.9 %copy-start.4 = (bf16[2,512]{1,0:T(2,128)(2,1)S(1)}, bf16[2,512]{1,0:T(2,128)(2,1)}, u32[]{:S(2)}) copy-start(bf16[2,512]{1,0:T(2,128)(2,1)} %ak_ref.1) | copy-start | bytes 6148
  0.7 0.9 %copy-start.5 = (bf16[2,512]{1,0:T(2,128)(2,1)S(1)}, bf16[2,512]{1,0:T(2,128)(2,1)}, u32[]{:S(2)}) copy-start(bf16[2,512]{1,0:T(2,128)(2,1)} %av_ref.1) | copy-start | bytes 6148
  1.7 4.6 %collective-permute-start.9 = (bf16[32,128]{1,0:T(8,128)(2,1)S(1)}, bf16[32,128]{1,0:T(8,128)(2,1)S(1)}, u32[]{:S(2)}, u32[]{:S(2)}) collective-permute-start(bf16[32,128]{1,0:T(8,128)(2,1)S(1)} %get-tuple-element.19), channel_id=1, source_target_pairs={{0,1},{1,0},{2,3},{3,2},{4,5},{5,4},{6,7},{7,6},{8,9},{9,8},{10,11... | collective-permute-start | bytes 24584 | tf_op jit(solution)/shard_map/ppermute | solution.py:300
  1.8 4.9 %collective-permute-start.10 = (bf16[32,128]{1,0:T(8,128)(2,1)S(1)}, bf16[32,128]{1,0:T(8,128)(2,1)S(1)}, u32[]{:S(2)}, u32[]{:S(2)}) collective-permute-start(bf16[32,128]{1,0:T(8,128)(2,1)S(1)} %get-tuple-element.20), channel_id=1, source_target_pairs={{0,2},{1,3},{2,0},{3,1},{4,6},{5,7},{6,4},{7,5},{8,10},{9,11},{10,... | collective-permute-start | bytes 24584 | tf_op jit(solution)/shard_map/ppermute | solution.py:300
  4.5 3.5 %collective-permute-start.11 = (bf16[32,128]{1,0:T(8,128)(2,1)S(1)}, bf16[32,128]{1,0:T(8,128)(2,1)S(1)}, u32[]{:S(2)}, u32[]{:S(2)}) collective-permute-start(bf16[32,128]{1,0:T(8,128)(2,1)S(1)} %get-tuple-element.21), channel_id=1, source_target_pairs={{0,3},{1,2},{2,1},{3,0},{4,7},{5,6},{6,5},{7,4},{8,11},{9,10},{10,... | collective-permute-start | bytes 24584 | tf_op jit(solution)/shard_map/ppermute | solution.py:300
  4.6 7.1 %collective-permute-start = (bf16[256,128]{1,0:T(8,128)(2,1)S(1)}, bf16[256,128]{1,0:T(8,128)(2,1)S(1)}, u32[]{:S(2)}, u32[]{:S(2)}) collective-permute-start(bf16[256,128]{1,0:T(8,128)(2,1)S(1)} %get-tuple-element.12), channel_id=1, source_target_pairs={{0,3},{1,2},{2,1},{3,0},{4,7},{5,6},{6,5},{7,4},{8,11},{9,10},{10,... | collective-permute-start | bytes 196616 | tf_op jit(solution)/shard_map/ppermute | solution.py:300
  6.3 5.4 %collective-permute-start.1 = (bf16[256,128]{1,0:T(8,128)(2,1)S(1)}, bf16[256,128]{1,0:T(8,128)(2,1)S(1)}, u32[]{:S(2)}, u32[]{:S(2)}) collective-permute-start(bf16[256,128]{1,0:T(8,128)(2,1)S(1)} %get-tuple-element.13), channel_id=1, source_target_pairs={{0,2},{1,3},{2,0},{3,1},{4,6},{5,7},{6,4},{7,5},{8,10},{9,11},{10,... | collective-permute-start | bytes 196616 | tf_op jit(solution)/shard_map/ppermute | solution.py:300
  6.3 5.0 %collective-permute-start.2 = (bf16[256,128]{1,0:T(8,128)(2,1)S(1)}, bf16[256,128]{1,0:T(8,128)(2,1)S(1)}, u32[]{:S(2)}, u32[]{:S(2)}) collective-permute-start(bf16[256,128]{1,0:T(8,128)(2,1)S(1)} %get-tuple-element.14), channel_id=1, source_target_pairs={{0,1},{1,0},{2,3},{3,2},{4,5},{5,4},{6,7},{7,6},{8,9},{9,8},{10,11... | collective-permute-start | bytes 196616 | tf_op jit(solution)/shard_map/ppermute | solution.py:300
  8.0 7.3 %collective-permute-start.14 = (bf16[80,128]{1,0:T(8,128)(2,1)S(1)}, bf16[80,128]{1,0:T(8,128)(2,1)S(1)}, u32[]{:S(2)}, u32[]{:S(2)}) collective-permute-start(bf16[80,128]{1,0:T(8,128)(2,1)S(1)} %regroup.1.in_ref.refs_0_), channel_id=1, source_target_pairs={{0,12},{1,13},{2,14},{3,15},{4,8},{5,9},{6,10},{7,11},{8,4},{9,5},... | collective-permute-start | bytes 61448 | tf_op jit(solution)/shard_map/ppermute | solution.py:303
  11.3 4.4 %collective-permute-start.13 = (bf16[80,128]{1,0:T(8,128)(2,1)S(1)}, bf16[80,128]{1,0:T(8,128)(2,1)S(1)}, u32[]{:S(2)}, u32[]{:S(2)}) collective-permute-start(bf16[80,128]{1,0:T(8,128)(2,1)S(1)} %regroup.1.in_ref.refs_0_), channel_id=1, source_target_pairs={{0,8},{1,9},{2,10},{3,11},{4,12},{5,13},{6,14},{7,15},{8,0},{9,1},... | collective-permute-start | bytes 61448 | tf_op jit(solution)/shard_map/ppermute | solution.py:303
  11.3 4.4 %collective-permute-start.12 = (bf16[80,128]{1,0:T(8,128)(2,1)S(1)}, bf16[80,128]{1,0:T(8,128)(2,1)S(1)}, u32[]{:S(2)}, u32[]{:S(2)}) collective-permute-start(bf16[80,128]{1,0:T(8,128)(2,1)S(1)} %again.1), channel_id=1, source_target_pairs={{0,4},{1,5},{2,6},{3,7},{4,0},{5,1},{6,2},{7,3},{8,12},{9,13},{10,... | collective-permute-start | bytes 61448 | tf_op jit(solution)/shard_map/ppermute | solution.py:303
  11.7 10.3 %collective-permute-start.5 = (bf16[256,128]{1,0:T(8,128)(2,1)S(1)}, bf16[256,128]{1,0:T(8,128)(2,1)S(1)}, u32[]{:S(2)}, u32[]{:S(2)}) collective-permute-start(bf16[256,128]{1,0:T(8,128)(2,1)S(1)} %select_select_fusion.1), channel_id=1, source_target_pairs={{0,4},{1,5},{2,6},{3,7},{4,0},{5,1},{6,2},{7,3},{8,12},{9,13},{10,... | collective-permute-start | bytes 196616 | tf_op jit(solution)/shard_map/ppermute | solution.py:310
  12.9 9.1 %collective-permute-start.4 = (bf16[256,128]{1,0:T(8,128)(2,1)S(1)}, bf16[256,128]{1,0:T(8,128)(2,1)S(1)}, u32[]{:S(2)}, u32[]{:S(2)}) collective-permute-start(bf16[256,128]{1,0:T(8,128)(2,1)S(1)} %select_select_fusion.1), channel_id=1, source_target_pairs={{0,8},{1,9},{2,10},{3,11},{4,0},{5,1},{6,2},{7,3},{8,12},{9,13},{1... | collective-permute-start | bytes 196616 | tf_op jit(solution)/shard_map/ppermute | solution.py:310
  15.2 6.8 %collective-permute-start.3 = (bf16[256,128]{1,0:T(8,128)(2,1)S(1)}, bf16[256,128]{1,0:T(8,128)(2,1)S(1)}, u32[]{:S(2)}, u32[]{:S(2)}) collective-permute-start(bf16[256,128]{1,0:T(8,128)(2,1)S(1)} %select_select_fusion.1), channel_id=1, source_target_pairs={{0,12},{1,13},{2,14},{3,15},{4,0},{5,1},{6,2},{7,3},{8,4},{9,5},{1... | collective-permute-start | bytes 196616 | tf_op jit(solution)/shard_map/ppermute | solution.py:310
  15.7 8.2 %copy-start = (bf16[128,4096]{1,0:T(8,128)(2,1)S(1)}, bf16[128,4096]{1,0:T(8,128)(2,1)}, u32[]{:S(2)}) copy-start(bf16[128,4096]{1,0:T(8,128)(2,1)} %q_ref.5) | copy-start | bytes 3145732
  17.2 13.6 %all-to-all-start = ((bf16[16,40,128]{2,1,0:T(8,128)(2,1)}), bf16[16,40,128]{2,1,0:T(8,128)(2,1)S(1)}, u32[]{:S(2)}, u32[]{:S(2)}) async-start(bf16[16,40,128]{2,1,0:T(8,128)(2,1)} %ask.1), calls=%async_computation | async-start | bytes 327680 | tf_op jit(solution)/shard_map/all_to_all | solution.py:346
  22.1 1.8 %collective-permute-start.7 = (bf16[256,128]{1,0:T(8,128)(2,1)S(1)}, bf16[256,128]{1,0:T(8,128)(2,1)S(1)}, u32[]{:S(2)}, u32[]{:S(2)}) collective-permute-start(bf16[256,128]{1,0:T(8,128)(2,1)S(1)} %select_select_fusion.refs_0_), channel_id=1, source_target_pairs={{0,1},{1,0},{2,3},{3,2},{4,5},{5,4},{6,7},{7,6},{8,9},{9,8},{10,11... | collective-permute-start | bytes 196616 | tf_op jit(solution)/shard_map/ppermute | solution.py:300
  22.4 4.3 %collective-permute-start.6 = (bf16[256,128]{1,0:T(8,128)(2,1)S(1)}, bf16[256,128]{1,0:T(8,128)(2,1)S(1)}, u32[]{:S(2)}, u32[]{:S(2)}) collective-permute-start(bf16[256,128]{1,0:T(8,128)(2,1)S(1)} %select_select_fusion.refs_0_), channel_id=1, source_target_pairs={{0,2},{1,3},{2,0},{3,1},{4,6},{5,7},{6,4},{7,5},{8,10},{9,11},{10,... | collective-permute-start | bytes 196616 | tf_op jit(solution)/shard_map/ppermute | solution.py:300
  26.7 2.1 %collective-permute-start.8 = (bf16[256,128]{1,0:T(8,128)(2,1)S(1)}, bf16[256,128]{1,0:T(8,128)(2,1)S(1)}, u32[]{:S(2)}, u32[]{:S(2)}) collective-permute-start(bf16[256,128]{1,0:T(8,128)(2,1)S(1)} %after.1.refs_0_), channel_id=1, source_target_pairs={{0,1},{1,0},{2,3},{3,2},{4,5},{5,4},{6,7},{7,6},{8,9},{9,8},{10,11... | collective-permute-start | bytes 196616 | tf_op jit(solution)/shard_map/ppermute | solution.py:300
